TPU v7x, 32 devices: a whole 2x2x4 slice. The times are simulated.
32 devices in a mesh: groups: 2 (over x), ops: 8 (over z, y), sec: 2 (over core).
Axes of the slice: x: 2, y: 2, z: 4, core: 2. Of those that a mesh axis runs over, the one named last changes fastest.
Arguments:
- wavefunction: bfloat16 [256, 8, 4096], P(None, ('groups', 'sec')), parts along dimension 1, may hold values from -6 to 6
- left_env: bfloat16 [128, 4, 256, 256], P(('groups', 'ops'), 'sec'), parts along dimension 0, may hold values from -0.375 to 0.375
- right_env: bfloat16 [128, 4, 256, 256], P(('groups', 'ops'), 'sec'), parts along dimension 0, may hold values from -0.046875 to 0.046875
- left_site_weight: float32 [12, 4, 4], replicated, may hold values from -3 to 3
- w_right: float32 [12, 4, 4], replicated, may hold values from -3 to 3
- term_id: int32 [128], P(('groups', 'ops')), parts along dimension 0, may hold values from 0 to 11
- left_sizes: int32 [8], P('groups'), parts along dimension 0, may hold values from 64 to 256, as said below
- right_sizes: int32 [8], P('groups'), parts along dimension 0, may hold values from 64 to 256, as said below
- sector_order: int32 [8], P('groups'), parts along dimension 0, may hold values from 0 to 3, as said below
Outputs:
- product: bfloat16 [256, 8, 4096], P('ops', ('groups', 'sec')), parts along dimension 1
There are 2 independent parts, one for each index of `groups`. A program takes and returns all parts, laid end to end along the dimension named above; an argument that names none is the same for every part. Nothing has to cross between parts.
Inputs may be any that keep to these rules, and one draw needn't show every extreme that they name: `left_sizes`: some sector of each part has exactly 256 left bond states. `right_sizes`: some sector of each part has exactly 256 right bond states. `sector_order`: a permutation of the sectors.
All inputs are finite; a program needn't handle non-finite values.
Results may differ from a plain program's by a relative error of at most 0.013.
Values may be sent and summed in bfloat16 or wider, within the bound.
A program may use at most 256 MiB of HBM per device.

v0:
```python
import jax
import jax.numpy as jnp
from jax import lax
from jax.sharding import PartitionSpec as P


def apply_mask(values, size_left, size_right, row_offset, bond, state_vectors):
    row_count = values.shape[0]
    slots = values.shape[1]
    row_index = row_offset + jnp.arange(row_count, dtype=jnp.int32)
    col_index = jnp.arange(bond, dtype=jnp.int32)
    keep_left = row_index[:, None] < size_left[None, :]
    keep_right = col_index[None, :] < size_right[:, None]
    keep = keep_left[:, :, None, None] & keep_right[None, :, None, :]
    shaped = values.reshape(row_count, slots, state_vectors, bond)
    return jnp.where(keep, shaped, jnp.zeros_like(shaped)).reshape(
        row_count, slots, state_vectors * bond
    )


def local(
    wavefunction,
    left_env,
    right_env,
    left_site_weight,
    w_right,
    term_id,
    left_sizes,
    right_sizes,
    sector_order,
):
    onsite_term_list = left_env.shape[0]
    local_slots = left_env.shape[1]
    bond = left_env.shape[2]
    state_vectors = wavefunction.shape[2] // bond
    operators = left_site_weight.shape[0]
    stored = lax.all_gather(wavefunction, "sec", axis=1, tiled=True)
    own_index = lax.axis_index("sec")
    own_sectors = lax.dynamic_slice_in_dim(sector_order, own_index * local_slots, local_slots)
    size_left = jnp.take(left_sizes, own_sectors)
    size_right = jnp.take(right_sizes, own_sectors)
    work = apply_mask(
        jnp.take(stored, own_sectors, axis=1), size_left, size_right, 0, bond, state_vectors
    )
    sector_picker = (term_id[:, None] == jnp.arange(operators, dtype=jnp.int32)[None, :]).astype(
        jnp.float32
    )
    left_operator_list = jnp.einsum(
        "fz,zyd->fyd", sector_picker, left_site_weight, precision=lax.Precision.HIGHEST
    )
    right_operator_list = jnp.einsum(
        "tn,nbd->tbd", sector_picker, w_right, precision=lax.Precision.HIGHEST
    )
    lookup_tables = jnp.einsum("ysz,yxe->ysxze", left_operator_list, right_operator_list).reshape(
        onsite_term_list, state_vectors, state_vectors
    )
    table_high = lookup_tables.astype(jnp.bfloat16)
    high_wide = lax.optimization_barrier(table_high).astype(jnp.float32)
    table_low = (lookup_tables - high_wide).astype(jnp.bfloat16)
    row_share = bond // lax.axis_size("ops")
    row_offset = lax.axis_index("ops") * row_share
    applied = jnp.einsum(
        "tklm,mkx->tklx", left_env, work, preferred_element_type=jnp.float32
    ).astype(jnp.bfloat16)
    shaped = applied.reshape(onsite_term_list, local_slots, bond, state_vectors, bond)
    mixed_high = jnp.einsum(
        "tpq,tklqr->tklpr", table_high, shaped, preferred_element_type=jnp.float32
    )
    mixed_low = jnp.einsum(
        "tpq,tklqr->tklpr", table_low, shaped, preferred_element_type=jnp.float32
    )
    mixed = (mixed_high + mixed_low).astype(jnp.bfloat16)
    term = jnp.einsum("tklpr,tkrs->lkps", mixed, right_env, preferred_element_type=jnp.float32)
    partial_value = term.reshape(bond, local_slots, state_vectors * bond)
    summed = lax.psum(partial_value.astype(jnp.bfloat16), "ops").astype(jnp.float32)
    own_rows = lax.dynamic_slice_in_dim(summed, row_offset, row_share, 0)
    return apply_mask(own_rows, size_left, size_right, row_offset, bond, state_vectors).astype(
        jnp.bfloat16
    )


def solution(mesh):
    return jax.shard_map(
        local,
        mesh=mesh,
        in_specs=(
            P(None, ("groups", "sec"), None),
            P(("groups", "ops"), "sec", None, None),
            P(("groups", "ops"), "sec", None, None),
            P(),
            P(),
            P(("groups", "ops")),
            P("groups"),
            P("groups"),
            P("groups"),
        ),
        out_specs=P("ops", ("groups", "sec"), None),
        check_vma=False,
    )
```

profile of v0, /device:TPU:0, one launch (start us, length us, event | category | flops | bytes accessed | tf_op | source)
XLA Modules:
  0.0 370.5 jit_solution(6045481877616686242)
XLA Ops:
  6.5 0.0 copy-start
  6.5 0.0 all-gather.2.cloned.1.call-start
  6.5 7.2 %copy.22 = bf16[256,2,4096]{2,0,1:T(8,128)(2,1)} copy(bf16[256,2,4096]{2,1,0:T(2,128)(2,1)} %param.11) | data formatting | bytes 8388608 | tf_op args[0]
  13.7 0.0 copy-start.5
  13.7 0.0 copy-start.2
  13.8 0.0 copy-start.3
  13.8 0.0 all-gather.2.cloned.1.call-update
  13.8 0.0 copy-start.6
  13.8 0.0 copy-start.8
  13.8 0.0 copy-start.7
  13.8 0.0 all-reduce.2.cloned.1.call-start
  13.9 0.5 copy-done.5
  14.4 0.1 compare_and_fusion
  14.5 0.0 copy-done.2
  14.5 0.6 gather_fusion.2
  15.1 0.0 copy-done.3
  15.1 0.6 gather_fusion.3
  15.8 0.1 iota_compare_fusion.3
  15.9 0.1 iota_compare_fusion.4
  15.9 0.1 broadcast_and_fusion
  16.1 0.9 broadcast_in_dim.57
  17.0 4.2 %copy.23 = pred[256,2,4096]{2,0,1:T(32,128)(4,1)} copy(pred[256,2,4096]{0,2,1:T(32,128)(4,1)S(1)} %bitcast.48) | data formatting | bytes 4194304 | tf_op jit(solution)/shard_map/jit(_where)/broadcast_in_dim | solution.py:16
  21.2 0.0 copy-done.6
  21.3 0.0 copy-done.8
  21.3 0.2 fusion.17
  21.4 0.0 copy-done.7
  21.5 0.2 fusion.16
  21.7 0.1 copy.34
  21.8 0.1 copy.35
  22.0 14.7 %all-gather.2.cloned.1.call-done = bf16[256,4,4096]{2,0,1:T(8,128)(2,1)} async-done(((bf16[256,2,4096]{2,0,1:T(8,128)(2,1)}), bf16[256,4,4096]{2,0,1:T(8,128)(2,1)}) %all-gather.2.cloned.1.call-update) | async-done | bytes 8388624 | tf_op jit(solution)/shard_map/all_gather | solution.py:37
  36.7 6.0 %fusion.23 = (bf16[256,4,2048]{2,0,1:T(8,128)(2,1)}, bf16[256,4,2048]{2,0,1:T(8,128)(2,1)}) fusion(bf16[256,4,4096]{2,0,1:T(8,128)(2,1)} %all-gather.2.cloned.1.call-done), kind=kLoop, calls=%fused_computation.43 | loop fusion | bytes 16777216 | tf_op jit(solution)/shard_map/jit(_take)/gather | solution.py:43
  42.7 4.2 %gather_fusion = bf16[2,256,2048]{2,1,0:T(8,128)(2,1)} fusion(bf16[256,4,2048]{2,0,1:T(8,128)(2,1)} %get-tuple-element.8, s32[1024]{0:T(1024)S(1)} %pad_clamp_fusion), kind=kCustom, calls=%fused_computation.2 | custom fusion | bytes 4194312 | tf_op jit(solution)/shard_map/jit(_take)/gather | solution.py:43
  46.9 4.2 %gather_fusion.1 = bf16[2,256,2048]{2,1,0:T(8,128)(2,1)} fusion(bf16[256,4,2048]{2,0,1:T(8,128)(2,1)} %get-tuple-element.9, s32[1024]{0:T(1024)S(1)} %pad_clamp_fusion), kind=kCustom, calls=%fused_computation.3 | custom fusion | bytes 4194312 | tf_op jit(solution)/shard_map/jit(_take)/gather | solution.py:43
  51.1 0.0 copy-done
  51.1 19.9 %convolution_convert_fusion = bf16[2,4096,8,256]{3,1,2,0:T(8,128)(2,1)} fusion(pred[256,2,4096]{2,0,1:T(32,128)(4,1)} %copy.23, bf16[256,2,2048]{2,0,1:T(8,128)(2,1)} %bitcast.47, bf16[256,2,2048]{2,0,1:T(8,128)(2,1)} %bitcast.46, pred[2]{0:T(512)(128)(4,1)S(1)} %get-tuple-element.6, bf16[8,2,256,256]{3,2,1,0:T(8,128)(2,1)S(1)} %copy-done), kind=kOutput, calls=%fused_computation.8 | convolution fusion | flops 8619294720 | bytes 41943040 | tf_op jit(solution)/shard_map/tklm,mkx->tklx/dot_general | solution.py:62
  71.0 44.8 %copy.26 = bf16[8,2,256,16,256]{4,3,2,1,0:T(8,128)(2,1)} copy(bf16[8,2,256,16,256]{2,4,3,0,1:T(8,128)(2,1)} %bitcast.44) | data formatting | bytes 67108864 | tf_op jit(solution)/shard_map/reshape | solution.py:65
  115.9 0.0 copy-start.4
  115.9 33.3 %fusion.24 = f32[8,2,256,256,16]{3,4,2,1,0:T(8,128)} fusion(bf16[8,16,16,1,1]{2,1,4,3,0:T(8,128)(2,1)S(1)} %copy.34, bf16[8,2,256,16,256]{4,3,2,1,0:T(8,128)(2,1)} %copy.26), kind=kOutput, calls=%fused_computation.44 | convolution fusion | flops 536870912 | bytes 100667392 | tf_op jit(solution)/shard_map/tpq,tklqr->tklpr/dot_general | solution.py:66
  149.2 0.0 copy-done.4
  149.2 35.2 %fusion.1 = bf16[2,256,16,256,1]{3,2,1,0,4:T(8,128)(2,1)} fusion(f32[8,2,256,256,16]{3,4,2,1,0:T(8,128)} %fusion.24, bf16[8,16,16,1,1]{2,1,4,3,0:T(8,128)(2,1)S(1)} %copy.35, bf16[8,2,256,16,256]{4,3,2,1,0:T(8,128)(2,1)} %copy.26, bf16[8,2,256,256]{3,2,1,0:T(8,128)(2,1)S(1)} %copy-done.4), kind=kOutput, calls=%fused_computation.6 | convolution fusion | flops 9160359936 | bytes 106958848 | tf_op jit(solution)/shard_map/tklpr,tkrs->lkps/dot_general | solution.py:73
  184.3 7.5 %copy.38 = bf16[2,256,16,256,1]{1,3,2,0,4:T(8,128)(2,1)} copy(bf16[2,256,16,256,1]{3,2,1,0,4:T(8,128)(2,1)} %fusion.1) | data formatting | bytes 8388608 | tf_op jit(solution)/shard_map/tklpr,tkrs->lkps/dot_general | solution.py:73
  191.8 0.0 copy-start.1
  191.8 11.4 %copy.32 = bf16[256,2,4096]{2,1,0:T(2,128)(2,1)} copy(bf16[256,2,4096]{0,2,1:T(8,128)(2,1)} %bitcast.45) | data formatting | bytes 8388608 | tf_op jit(solution)/shard_map/convert_element_type | solution.py:75
  203.2 0.0 all-reduce.2.cloned.1.call-update
  203.3 0.1 broadcast_compare_fusion
  203.3 0.1 broadcast_and_fusion.1
  203.5 0.1 broadcast_in_dim.55
  203.5 0.4 broadcast_in_dim.56
  203.9 157.0 %all-reduce.2.cloned.1.call-done = bf16[256,2,4096]{2,1,0:T(2,128)(2,1)} async-done(((bf16[256,2,4096]{2,1,0:T(2,128)(2,1)}), bf16[256,2,4096]{2,1,0:T(2,128)(2,1)}) %all-reduce.2.cloned.1.call-update) | async-done | bytes 4194320 | tf_op jit(solution)/shard_map/psum | solution.py:75
  360.9 2.8 select_convert_fusion
  363.7 0.0 copy-done.1
  (7 shorter events, 0.1 us)
Async XLA Ops:
  6.5 44.6 %copy-start = (bf16[8,2,256,256]{3,2,1,0:T(8,128)(2,1)S(1)}, bf16[8,2,256,256]{3,2,1,0:T(8,128)(2,1)}, u32[]{:S(2)}) copy-start(bf16[8,2,256,256]{3,2,1,0:T(8,128)(2,1)} %param.12) | copy-start | bytes 6291460
  6.5 30.1 %all-gather.2.cloned.1.call-start = ((), (), s32[]{:S(2)}) async-start(), calls=%async_computation | async-start | bytes 12582912 | tf_op jit(solution)/shard_map/all_gather | solution.py:37
  13.7 0.7 copy-start.5
  13.7 0.7 copy-start.2
  13.8 1.4 copy-start.3
  13.8 7.5 %copy-start.6 = (f32[12,4,4]{0,2,1:T(4,128)S(1)}, f32[12,4,4]{0,2,1:T(4,128)}, u32[]{:S(2)}) copy-start(f32[12,4,4]{0,2,1:T(4,128)} %param.15) | copy-start | bytes 2308
  13.8 7.5 %copy-start.8 = (s32[8]{0:T(128)S(1)}, s32[8]{0:T(128)}, u32[]{:S(2)}) copy-start(s32[8]{0:T(128)} %param.16) | copy-start | bytes 100
  13.8 7.7 %copy-start.7 = (f32[12,4,4]{0,2,1:T(4,128)S(1)}, f32[12,4,4]{0,2,1:T(4,128)}, u32[]{:S(2)}) copy-start(f32[12,4,4]{0,2,1:T(4,128)} %param.14) | copy-start | bytes 2308
  13.8 347.1 %all-reduce.2.cloned.1.call-start = ((), (), s32[]{:S(2)}) async-start(), calls=%async_computation.1 | async-start | bytes 8388608 | tf_op jit(solution)/shard_map/psum | solution.py:75
  115.9 33.3 %copy-start.4 = (bf16[8,2,256,256]{3,2,1,0:T(8,128)(2,1)S(1)}, bf16[8,2,256,256]{3,2,1,0:T(8,128)(2,1)}, u32[]{:S(2)}) copy-start(bf16[8,2,256,256]{3,2,1,0:T(8,128)(2,1)} %param.13) | copy-start | bytes 6291460
  191.8 171.8 %copy-start.1 = (bf16[8,2,256,256]{3,2,1,0:T(8,128)(2,1)S(1)}, bf16[8,2,256,256]{3,2,1,0:T(8,128)(2,1)}, u32[]{:S(2)}) copy-start(bf16[8,2,256,256]{3,2,1,0:T(8,128)(2,1)} %param.12) | copy-start | bytes 6291460
Sparse Core Ops, SparseCore 0:
  13.9 22.7 all-gather.1
  203.4 157.4 all-reduce.1
where the time goes:
time: 372 us; the launch traced here: 370 us
  waiting for transfers between devices  172 us (46%)
  local copies, waits for them, and re-layouts  93 us (25%)
  matrix products  88.8 us (24%)
  between operations  13.5 us (4%)
    psum x1, waiting for transfers between devices, local(): lax.psum(partial_value.astype(jnp.bfloat16), 'ops').astype(jnp.float32)  157 us
    reshape x1, local copies, waits for them, and re-layouts, local(): applied.reshape(onsite_term_list, local_slots, bond, state_vectors, bond)  44.8 us
    dot_general x1, matrix products, local(): jnp.einsum('tklpr,tkrs->lkps', mixed, right_env, preferred_element_type=j...  35.2 us
    dot_general x1, matrix products, local(): jnp.einsum('tpq,tklqr->tklpr', table_high, shaped, preferred_element_type...  33.3 us
    dot_general x1, matrix products, local(): jnp.einsum('tklm,mkx->tklx', left_env, work, preferred_element_type=jnp.f...  19.9 us
    all_gather x1, waiting for transfers between devices, local(): stored = lax.all_gather(wavefunction, 'sec', axis=1, tiled=True)  14.7 us
    gather x3, local copies, waits for them, and re-layouts, local(): jnp.take(stored, own_sectors, axis=1)  14.4 us
    convert_element_type x1, local copies, waits for them, and re-layouts, local(): partial_value.astype(jnp.bfloat16)  11.4 us
  transfers between devices with their start and end apart: 2, of which 2 were waited for; matrix products, arithmetic and copies ran while one was open for 2% of the time, Pallas kernels for 0%

commit v1 on v0

v1 whole, which is shorter than its diff:
```python
import functools

import jax
import jax.numpy as jnp
from jax import lax
from jax.experimental import pallas as pl
from jax.experimental.pallas import tpu as pltpu
from jax.sharding import PartitionSpec as P

MESH = pl.DeviceIdType.MESH
SUB = 16
INNER = 2
CHUNKS = 4


def kernel(
    dims,
    wave,
    left,
    right,
    table,
    order_ref,
    left_size_ref,
    right_size_ref,
    out,
    *scratch,
):
    terms, slots, bond, states, ops = dims
    chunk_bufs = scratch[:CHUNKS]
    (
        left_v,
        right_v,
        kron,
        applied,
        mixed,
        own_part,
        pair_out,
        pair_in,
        line_out,
        line_in,
        wave_local_sem,
        wave_send_sem,
        wave_recv_sem,
        env_sem,
        pair_send_sem,
        pair_recv_sem,
        line_send_sem,
        line_recv_sem,
    ) = scratch[CHUNKS:]
    outer = ops // INNER
    blocks = bond // ops // SUB
    steps = slots * outer
    tile = states * SUB
    wide = states * bond // CHUNKS
    per_chunk = states // CHUNKS

    group = lax.axis_index("groups")
    op = lax.axis_index("ops")
    sec = lax.axis_index("sec")
    far = lax.div(op, INNER)
    near = lax.rem(op, INNER)
    other_sec = 1 - sec
    pair_id = (group, far * INNER + (1 - near), sec)
    sec_id = (group, op, other_sec)

    barrier = pltpu.get_barrier_semaphore()
    pl.semaphore_signal(barrier, inc=1, device_id=sec_id, device_id_type=MESH)
    pl.semaphore_signal(barrier, inc=1, device_id=pair_id, device_id_type=MESH)
    for hop in range(1, outer):
        peer = lax.rem(far + hop, outer) * INNER + near
        pl.semaphore_signal(barrier, inc=1, device_id=(group, peer, sec), device_id_type=MESH)
    pl.semaphore_wait(barrier, outer + 1)

    base = sec * slots
    wave_copies = []
    for c in range(CHUNKS):
        source = wave.at[:, :, pl.ds(c * wide, wide)]
        target = chunk_bufs[c].at[pl.ds(base, slots)]
        sent = pltpu.make_async_remote_copy(
            src_ref=source,
            dst_ref=target,
            send_sem=wave_send_sem.at[c],
            recv_sem=wave_recv_sem.at[c],
            device_id=sec_id,
            device_id_type=MESH,
        )
        sent.start()
        kept = pltpu.make_async_copy(source, target, wave_local_sem.at[c])
        kept.start()
        wave_copies.append((sent, kept))
    left_copy = pltpu.make_async_copy(left, left_v, env_sem.at[0])
    left_copy.start()
    right_copy = pltpu.make_async_copy(right, right_v, env_sem.at[1])
    right_copy.start()

    row = lax.broadcasted_iota(jnp.int32, (tile, tile), 0)
    col = lax.broadcasted_iota(jnp.int32, (tile, tile), 1)
    same = (row & (SUB - 1)) == (col & (SUB - 1))
    row_state = lax.broadcasted_iota(jnp.int32, (tile, states), 0) >> 4
    spread = (row_state == lax.broadcasted_iota(jnp.int32, (tile, states), 1)).astype(jnp.bfloat16)
    col_state = lax.broadcasted_iota(jnp.int32, (states, tile), 1) >> 4
    spread_t = (col_state == lax.broadcasted_iota(jnp.int32, (states, tile), 0)).astype(
        jnp.bfloat16
    )
    for t in range(terms):
        tall = jnp.dot(spread, table[t], preferred_element_type=jnp.float32).astype(jnp.bfloat16)
        full = jnp.dot(tall, spread_t, preferred_element_type=jnp.float32)
        kron[t] = jnp.where(same, full, 0.0).astype(jnp.bfloat16)
    left_copy.wait()
    right_copy.wait()

    mask_row = lax.broadcasted_iota(jnp.int32, (bond, bond), 0)
    mask_col = lax.broadcasted_iota(jnp.int32, (bond, bond), 1)

    def apply_left(k, first):
        sector = order_ref[base + k]
        keep = (mask_row < left_size_ref[sector]) & (mask_col < right_size_ref[sector])
        keep = jnp.where(keep, 1.0, 0.0).astype(jnp.bfloat16)
        for c in range(CHUNKS):

            @pl.when(first)
            def _():
                sent, kept = wave_copies[c]
                kept.wait()
                sent.wait_recv()

            @pl.loop(0, per_chunk)
            def _(i):
                lanes = pl.ds(pl.multiple_of(i * bond, bond), bond)
                block = chunk_bufs[c][sector, :, lanes] * keep
                at = pl.ds(pl.multiple_of((c * per_chunk + i) * SUB, SUB), SUB)
                for t in range(0, terms, 2):
                    lhs = left_v[pl.ds(t, 2), k].reshape(2 * bond, bond)
                    res = jnp.dot(lhs, block, preferred_element_type=jnp.float32)
                    res = res.astype(jnp.bfloat16).reshape(2, bond // SUB, SUB, bond)
                    applied[pl.ds(t, 2), :, at, :] = res

    def rows_for(k, dest):
        for b in range(blocks):
            for t in range(terms):
                res = jnp.dot(
                    kron[t], applied[t, dest * blocks + b], preferred_element_type=jnp.float32
                )
                mixed[pl.ds(b * tile, tile), pl.ds(t * bond, bond)] = res.astype(jnp.bfloat16)
        flat = right_v[:, k].reshape(terms * bond, bond)
        return jnp.dot(mixed[...], flat, preferred_element_type=jnp.float32)

    def pair_copy(i):
        return pltpu.make_async_remote_copy(
            src_ref=pair_out.at[i],
            dst_ref=pair_in.at[i],
            send_sem=pair_send_sem.at[i],
            recv_sem=pair_recv_sem.at[i],
            device_id=pair_id,
            device_id_type=MESH,
        )

    def line_copy(i):
        peer = lax.rem(far + 1 + lax.rem(i, outer), outer) * INNER + near
        return pltpu.make_async_remote_copy(
            src_ref=line_out.at[i],
            dst_ref=line_in.at[i],
            send_sem=line_send_sem.at[i],
            recv_sem=line_recv_sem.at[i],
            device_id=(group, peer, sec),
            device_id_type=MESH,
        )

    def combine(i):
        pair_copy(i).wait_recv()

        @pl.when(lax.rem(i, outer) < outer - 1)
        def _():
            line_out[i] = (own_part[i] + pair_in[i].astype(jnp.float32)).astype(jnp.bfloat16)
            line_copy(i).start()

    def step(i, carry):
        k = lax.div(i, outer)
        j = lax.rem(i, outer)

        @pl.when(j == 0)
        def _():
            apply_left(k, i == 0)

        dest = lax.rem(far + 1 + j, outer) * INNER
        pair_out[i] = rows_for(k, dest + (1 - near)).astype(jnp.bfloat16)
        pair_copy(i).start()
        own_part[i] = rows_for(k, dest + near)

        @pl.when(i >= 1)
        def _():
            combine(i - 1)

        return carry

    lax.fori_loop(0, steps, step, 0)
    combine(steps - 1)

    out_row = lax.broadcasted_iota(jnp.int32, (SUB, bond), 0)
    out_col = lax.broadcasted_iota(jnp.int32, (SUB, bond), 1)
    for k in range(slots):
        mine = k * outer + outer - 1
        for j in range(outer - 1):
            line_copy(k * outer + j).wait_recv()
        sector = order_ref[base + k]
        size_left = left_size_ref[sector]
        size_right = right_size_ref[sector]
        for b in range(blocks):
            keep = (out_row + (op * blocks + b) * SUB < size_left) & (out_col < size_right)
            for p in range(states):
                rows = pl.ds(b * tile + p * SUB, SUB)
                total = own_part[mine, rows] + pair_in[mine, rows].astype(jnp.float32)
                for j in range(outer - 1):
                    total = total + line_in[k * outer + j, rows].astype(jnp.float32)
                out[k, pl.ds(b * SUB, SUB), pl.ds(p * bond, bond)] = jnp.where(
                    keep, total, 0.0
                ).astype(jnp.bfloat16)

    for sent, _ in wave_copies:
        sent.wait_send()

    def drain(i, carry):
        pair_copy(i).wait_send()

        @pl.when(lax.rem(i, outer) < outer - 1)
        def _():
            line_copy(i).wait_send()

        return carry

    lax.fori_loop(0, steps, drain, 0)


def local(
    wavefunction,
    left_env,
    right_env,
    left_site_weight,
    w_right,
    term_id,
    left_sizes,
    right_sizes,
    sector_order,
):
    terms, slots, bond = left_env.shape[0], left_env.shape[1], left_env.shape[2]
    states = wavefunction.shape[2] // bond
    ops = lax.axis_size("ops")
    sectors = slots * lax.axis_size("sec")
    operators = left_site_weight.shape[0]
    picker = (term_id[:, None] == jnp.arange(operators, dtype=jnp.int32)[None, :]).astype(
        jnp.float32
    )
    left_ops = jnp.einsum(
        "tn,nac->tac", picker, left_site_weight, precision=lax.Precision.HIGHEST
    )
    right_ops = jnp.einsum("tn,nbd->tbd", picker, w_right, precision=lax.Precision.HIGHEST)
    table = (
        (left_ops[:, :, None, :, None] * right_ops[:, None, :, None, :])
        .reshape(terms, states, states)
        .astype(jnp.bfloat16)
    )
    wave = jnp.transpose(wavefunction, (1, 0, 2))
    outer = ops // INNER
    steps = slots * outer
    share = bond // ops
    rows = share * states
    bf16 = jnp.bfloat16
    any_spec = pl.BlockSpec(memory_space=pl.ANY)
    vmem_spec = pl.BlockSpec(memory_space=pltpu.VMEM)
    smem_spec = pl.BlockSpec(memory_space=pltpu.SMEM)
    result = pl.pallas_call(
        functools.partial(kernel, (terms, slots, bond, states, ops)),
        out_shape=jax.ShapeDtypeStruct((slots, share, states * bond), bf16),
        in_specs=[any_spec, any_spec, any_spec, vmem_spec, smem_spec, smem_spec, smem_spec],
        out_specs=vmem_spec,
        scratch_shapes=[
            pltpu.VMEM((sectors, bond, states * bond // CHUNKS), bf16) for _ in range(CHUNKS)
        ]
        + [
            pltpu.VMEM((terms, slots, bond, bond), bf16),
            pltpu.VMEM((terms, slots, bond, bond), bf16),
            pltpu.VMEM((terms, states * SUB, states * SUB), bf16),
            pltpu.VMEM((terms, bond // SUB, states * SUB, bond), bf16),
            pltpu.VMEM((rows, terms * bond), bf16),
            pltpu.VMEM((steps, rows, bond), jnp.float32),
            pltpu.VMEM((steps, rows, bond), bf16),
            pltpu.VMEM((steps, rows, bond), bf16),
            pltpu.VMEM((steps, rows, bond), bf16),
            pltpu.VMEM((steps, rows, bond), bf16),
            pltpu.SemaphoreType.DMA((CHUNKS,)),
            pltpu.SemaphoreType.DMA((CHUNKS,)),
            pltpu.SemaphoreType.DMA((CHUNKS,)),
            pltpu.SemaphoreType.DMA((2,)),
            pltpu.SemaphoreType.DMA((steps,)),
            pltpu.SemaphoreType.DMA((steps,)),
            pltpu.SemaphoreType.DMA((steps,)),
            pltpu.SemaphoreType.DMA((steps,)),
        ],
        compiler_params=pltpu.CompilerParams(
            collective_id=0, has_side_effects=True, vmem_limit_bytes=56 * 1024 * 1024
        ),
        cost_estimate=pl.CostEstimate(
            flops=6 * terms * slots * states * bond**3, bytes_accessed=2**24, transcendentals=0
        ),
    )(wave, left_env, right_env, table, sector_order, left_sizes, right_sizes)
    return jnp.transpose(result, (1, 0, 2))


def solution(mesh):
    return jax.shard_map(
        local,
        mesh=mesh,
        in_specs=(
            P(None, ("groups", "sec"), None),
            P(("groups", "ops"), "sec", None, None),
            P(("groups", "ops"), "sec", None, None),
            P(),
            P(),
            P(("groups", "ops")),
            P("groups"),
            P("groups"),
            P("groups"),
        ),
        out_specs=P("ops", ("groups", "sec"), None),
        check_vma=False,
    )
```

time: 372 us -> 87.6 us (0.24)
  waiting for transfers between devices: 172 us -> 0 us
  matrix products: 88.8 us -> 1.74 us
  local copies, waits for them, and re-layouts: 93 us -> 10.8 us
  Pallas kernels: 0 us -> 73.7 us
  between operations: 13.5 us -> 0.02 us
    psum x1 -> x0, waiting for transfers between devices: 157 us -> none  [local(): lax.psum(partial_value.astype(jnp.bfloat16), 'ops').astype(jnp.float32)]
    dot_general x3 -> x0, matrix products: 88.4 us -> none  [the longest x1 35.2 us: local(): jnp.einsum('tklpr,tkrs->lkps', mixed, right_env, preferred_element_type=j...]
    pallas_call x0 -> x1, Pallas kernels: none -> 73.7 us  [local(): pl.pallas_call(functools.partial(kernel, (terms, slots, bond, states, ops...]
    reshape x1 -> x0, local copies, waits for them, and re-layouts: 44.8 us -> none  [local(): applied.reshape(onsite_term_list, local_slots, bond, state_vectors, bond)]
    gather x5 -> x0, local copies, waits for them, and re-layouts: 15.7 us -> none  [the longest x3 14.4 us: local(): jnp.take(stored, own_sectors, axis=1)]
    all_gather x1 -> x0, waiting for transfers between devices: 14.7 us -> none  [local(): stored = lax.all_gather(wavefunction, 'sec', axis=1, tiled=True)]
    convert_element_type x3 -> x1, local copies, waits for them, and re-layouts: 11.6 us -> 0.72 us  [local(): table = (left_ops[:, :, None, :, None] * right_ops[:, None, :, None, :])....]
    dot_general x1 -> x0, local copies, waits for them, and re-layouts: 7.5 us -> none  [local(): jnp.einsum('tklpr,tkrs->lkps', mixed, right_env, preferred_element_type=j...]
  transfers between devices with their start and end apart: 2 -> 0, of which waited for: 2 -> 0; matrix products, arithmetic and copies ran while one was open for 2% -> 0% of each run, Pallas kernels for 0% -> 0%
where the time goes in v1:
time: 87.6 us; the launch traced here: 86.4 us
  Pallas kernels  73.7 us (84%)
  local copies, waits for them, and re-layouts  10.8 us (12%)
  matrix products  1.74 us (2%)
    pallas_call x1, Pallas kernels, local(): pl.pallas_call(functools.partial(kernel, (terms, slots, bond, states, ops...  73.7 us
    unnamed x3, local copies, waits for them, and re-layouts  7.73 us
    transpose x1, local copies, waits for them, and re-layouts, local(): return jnp.transpose(result, (1, 0, 2))  2.38 us

profile of v1, /device:TPU:0, one launch (start us, length us, event | category | flops | bytes accessed | tf_op | source)
XLA Modules:
  0.0 86.4 jit_solution(2163745907873062040)
XLA Ops:
  0.0 0.0 copy-start
  0.0 0.7 copy-done
  0.7 0.8 fusion.1
  1.5 0.9 %fusion = f32[8,16]{0,1:S(1)} fusion(f32[12,16]{0,1:T(8,128)} %bitcast.17, s32[8]{0:T(128)} %param.14), kind=kOutput, calls=%fused_computation.3 | convolution fusion | flops 18528 | bytes 1312
  2.5 0.7 copy.15.table
  3.2 7.0 %copy.18 = bf16[256,2,4096]{2,0,1:T(8,128)(2,1)} copy(bf16[256,2,4096]{2,1,0:T(2,128)(2,1)} %param.9) | data formatting | bytes 8388608 | tf_op args[0]
  10.2 73.7 %shard_map.91 = bf16[2,32,4096]{2,1,0:T(8,128)(2,1)} custom-call(bf16[2,256,4096]{2,1,0:T(8,128)(2,1)} %bitcast.12, bf16[8,2,256,256]{3,2,1,0:T(8,128)(2,1)} %left.1, bf16[8,2,256,256]{3,2,1,0:T(8,128)(2,1)} %right.1, bf16[8,16,16]{2,1,0:T(8,128)(2,1)} %copy.15.table, s32[4]{0:T(128)} %order_ref.1, s32[4]{0:T(128)} %left_size_ref.1, s32[4]{0:T(128)} %right_size_ref.1), custom_call_target="tpu_custom_call" | custom-call | flops 25769803776 | bytes 16777216 | tf_op jit(solution)/shard_map/pallas_call | solution.py:271
  84.0 2.4 %copy.16 = bf16[32,2,4096]{2,1,0:T(2,128)(2,1)} copy(bf16[32,2,4096]{2,0,1:T(8,128)(2,1)} %bitcast.13) | data formatting | bytes 1048576 | tf_op jit(solution)/shard_map/transpose | solution.py:306
  (1 shorter events, 0.0 us)
Async XLA Ops:
  0.0 0.7 copy-start

commit v2 on v1

--- a/solution.py
+++ b/solution.py
@@ -18,7 +18,9 @@
     wave,
     left,
     right,
-    table,
+    left_op,
+    right_op,
+    term_ref,
     order_ref,
     left_size_ref,
     right_size_ref,
@@ -31,6 +33,7 @@
         left_v,
         right_v,
         kron,
+        work,
         applied,
         mixed,
         own_part,
@@ -51,6 +54,7 @@
     blocks = bond // ops // SUB
     steps = slots * outer
     tile = states * SUB
+    pair_rows = INNER * blocks * SUB
     wide = states * bond // CHUNKS
     per_chunk = states // CHUNKS
 
@@ -102,8 +106,28 @@
     spread_t = (col_state == lax.broadcasted_iota(jnp.int32, (states, tile), 0)).astype(
         jnp.bfloat16
     )
+    side = left_op.shape[1]
+    fine = lax.broadcasted_iota(jnp.int32, (states, side), 0)
+    which = lax.broadcasted_iota(jnp.int32, (states, side), 1)
+    fine_t = lax.broadcasted_iota(jnp.int32, (side, states), 1)
+    which_t = lax.broadcasted_iota(jnp.int32, (side, states), 0)
+
+    def widen(small, by_row, by_col):
+        rows = by_row.astype(jnp.float32)
+        cols = by_col.astype(jnp.float32)
+        tall = jnp.dot(
+            rows, small, precision=lax.Precision.HIGHEST, preferred_element_type=jnp.float32
+        )
+        return jnp.dot(
+            tall, cols, precision=lax.Precision.HIGHEST, preferred_element_type=jnp.float32
+        )
+
     for t in range(terms):
-        tall = jnp.dot(spread, table[t], preferred_element_type=jnp.float32).astype(jnp.bfloat16)
+        index = term_ref[t]
+        from_left = widen(left_op[index], (fine >> 2) == which, (fine_t >> 2) == which_t)
+        from_right = widen(right_op[index], (fine & 3) == which, (fine_t & 3) == which_t)
+        table = (from_left * from_right).astype(jnp.bfloat16)
+        tall = jnp.dot(spread, table, preferred_element_type=jnp.float32).astype(jnp.bfloat16)
         full = jnp.dot(tall, spread_t, preferred_element_type=jnp.float32)
         kron[t] = jnp.where(same, full, 0.0).astype(jnp.bfloat16)
     left_copy.wait()
@@ -112,10 +136,9 @@
     mask_row = lax.broadcasted_iota(jnp.int32, (bond, bond), 0)
     mask_col = lax.broadcasted_iota(jnp.int32, (bond, bond), 1)
 
-    def apply_left(k, first):
+    def apply_left(k, first, fresh, dest):
         sector = order_ref[base + k]
-        keep = (mask_row < left_size_ref[sector]) & (mask_col < right_size_ref[sector])
-        keep = jnp.where(keep, 1.0, 0.0).astype(jnp.bfloat16)
+        at_rows = pl.ds(pl.multiple_of(dest * blocks * SUB, SUB), pair_rows)
         for c in range(CHUNKS):
 
             @pl.when(first)
@@ -124,22 +147,28 @@
                 kept.wait()
                 sent.wait_recv()
 
-            @pl.loop(0, per_chunk)
-            def _(i):
-                lanes = pl.ds(pl.multiple_of(i * bond, bond), bond)
-                block = chunk_bufs[c][sector, :, lanes] * keep
-                at = pl.ds(pl.multiple_of((c * per_chunk + i) * SUB, SUB), SUB)
-                for t in range(0, terms, 2):
-                    lhs = left_v[pl.ds(t, 2), k].reshape(2 * bond, bond)
-                    res = jnp.dot(lhs, block, preferred_element_type=jnp.float32)
-                    res = res.astype(jnp.bfloat16).reshape(2, bond // SUB, SUB, bond)
-                    applied[pl.ds(t, 2), :, at, :] = res
-
-    def rows_for(k, dest):
+            @pl.when(fresh)
+            def _():
+                keep = (mask_row < left_size_ref[sector]) & (mask_col < right_size_ref[sector])
+                keep = jnp.where(keep, 1.0, 0.0).astype(jnp.bfloat16)
+                for i in range(per_chunk):
+                    lanes = pl.ds(i * bond, bond)
+                    work[c * per_chunk + i] = chunk_bufs[c][sector, :, lanes] * keep
+
+            @pl.loop(c * per_chunk, (c + 1) * per_chunk)
+            def _(q):
+                lhs = left_v[:, k, at_rows, :].reshape(terms * pair_rows, bond)
+                res = jnp.dot(lhs, work[q], preferred_element_type=jnp.float32)
+                at = pl.ds(pl.multiple_of(q * SUB, SUB), SUB)
+                applied[:, :, at, :] = res.astype(jnp.bfloat16).reshape(
+                    terms, INNER * blocks, SUB, bond
+                )
+
+    def rows_for(k, half):
         for b in range(blocks):
             for t in range(terms):
                 res = jnp.dot(
-                    kron[t], applied[t, dest * blocks + b], preferred_element_type=jnp.float32
+                    kron[t], applied[t, half * blocks + b], preferred_element_type=jnp.float32
                 )
                 mixed[pl.ds(b * tile, tile), pl.ds(t * bond, bond)] = res.astype(jnp.bfloat16)
         flat = right_v[:, k].reshape(terms * bond, bond)
@@ -178,14 +207,10 @@
         k = lax.div(i, outer)
         j = lax.rem(i, outer)
 
-        @pl.when(j == 0)
-        def _():
-            apply_left(k, i == 0)
-
-        dest = lax.rem(far + 1 + j, outer) * INNER
-        pair_out[i] = rows_for(k, dest + (1 - near)).astype(jnp.bfloat16)
+        apply_left(k, i == 0, j == 0, lax.rem(far + 1 + j, outer) * INNER)
+        pair_out[i] = rows_for(k, 1 - near).astype(jnp.bfloat16)
         pair_copy(i).start()
-        own_part[i] = rows_for(k, dest + near)
+        own_part[i] = rows_for(k, near)
 
         @pl.when(i >= 1)
         def _():
@@ -246,19 +271,6 @@
     states = wavefunction.shape[2] // bond
     ops = lax.axis_size("ops")
     sectors = slots * lax.axis_size("sec")
-    operators = left_site_weight.shape[0]
-    picker = (term_id[:, None] == jnp.arange(operators, dtype=jnp.int32)[None, :]).astype(
-        jnp.float32
-    )
-    left_ops = jnp.einsum(
-        "tn,nac->tac", picker, left_site_weight, precision=lax.Precision.HIGHEST
-    )
-    right_ops = jnp.einsum("tn,nbd->tbd", picker, w_right, precision=lax.Precision.HIGHEST)
-    table = (
-        (left_ops[:, :, None, :, None] * right_ops[:, None, :, None, :])
-        .reshape(terms, states, states)
-        .astype(jnp.bfloat16)
-    )
     wave = jnp.transpose(wavefunction, (1, 0, 2))
     outer = ops // INNER
     steps = slots * outer
@@ -271,7 +283,7 @@
     result = pl.pallas_call(
         functools.partial(kernel, (terms, slots, bond, states, ops)),
         out_shape=jax.ShapeDtypeStruct((slots, share, states * bond), bf16),
-        in_specs=[any_spec, any_spec, any_spec, vmem_spec, smem_spec, smem_spec, smem_spec],
+        in_specs=[any_spec] * 3 + [vmem_spec] * 2 + [smem_spec] * 4,
         out_specs=vmem_spec,
         scratch_shapes=[
             pltpu.VMEM((sectors, bond, states * bond // CHUNKS), bf16) for _ in range(CHUNKS)
@@ -280,7 +292,8 @@
             pltpu.VMEM((terms, slots, bond, bond), bf16),
             pltpu.VMEM((terms, slots, bond, bond), bf16),
             pltpu.VMEM((terms, states * SUB, states * SUB), bf16),
-            pltpu.VMEM((terms, bond // SUB, states * SUB, bond), bf16),
+            pltpu.VMEM((states, bond, bond), bf16),
+            pltpu.VMEM((terms, INNER * share // SUB, states * SUB, bond), bf16),
             pltpu.VMEM((rows, terms * bond), bf16),
             pltpu.VMEM((steps, rows, bond), jnp.float32),
             pltpu.VMEM((steps, rows, bond), bf16),
@@ -302,7 +315,17 @@
         cost_estimate=pl.CostEstimate(
             flops=6 * terms * slots * states * bond**3, bytes_accessed=2**24, transcendentals=0
         ),
-    )(wave, left_env, right_env, table, sector_order, left_sizes, right_sizes)
+    )(
+        wave,
+        left_env,
+        right_env,
+        left_site_weight,
+        w_right,
+        term_id,
+        sector_order,
+        left_sizes,
+        right_sizes,
+    )
     return jnp.transpose(result, (1, 0, 2))
 
 

time: 87.6 us -> 91.3 us (1.042); the launches traced: 86.4 us -> 91 us
  Pallas kernels: 73.7 us -> 78.8 us
  matrix products: 1.74 us -> 0 us
  local copies, waits for them, and re-layouts: 10.8 us -> 12.2 us
    pallas_call x1, Pallas kernels: 73.7 us -> 78.8 us  [local(): pl.pallas_call(functools.partial(kernel, (terms, slots, bond, states, ops...]
    unnamed x3, local copies, waits for them, and re-layouts: 7.73 us -> 9.82 us
    unnamed x2 -> x0, matrix products: 1.74 us -> none
where the time goes in v2:
time: 91.3 us; the launch traced here: 91 us
  Pallas kernels  78.8 us (86%)
  local copies, waits for them, and re-layouts  12.2 us (13%)
    pallas_call x1, Pallas kernels, local(): pl.pallas_call(functools.partial(kernel, (terms, slots, bond, states, ops...  78.8 us
    unnamed x3, local copies, waits for them, and re-layouts  9.82 us
    transpose x1, local copies, waits for them, and re-layouts, local(): return jnp.transpose(result, (1, 0, 2))  2.38 us

profile of v2, /device:TPU:0, one launch (start us, length us, event | category | flops | bytes accessed | tf_op | source)
XLA Modules:
  0.0 91.0 jit_solution(578617887677319424)
XLA Ops:
  0.0 1.4 %copy.11.left_op = f32[12,4,4]{2,1,0:T(4,128)} copy(f32[12,4,4]{0,2,1:T(4,128)} %param.12) | data formatting | bytes 1536 | tf_op args[3]
  1.4 1.4 %copy.12.right_op = f32[12,4,4]{2,1,0:T(4,128)} copy(f32[12,4,4]{0,2,1:T(4,128)} %param.13) | data formatting | bytes 1536 | tf_op args[4]
  2.8 7.0 %copy.15 = bf16[256,2,4096]{2,0,1:T(8,128)(2,1)} copy(bf16[256,2,4096]{2,1,0:T(2,128)(2,1)} %param.9) | data formatting | bytes 8388608 | tf_op args[0]
  9.8 78.8 %shard_map.91 = bf16[2,32,4096]{2,1,0:T(8,128)(2,1)} custom-call(bf16[2,256,4096]{2,1,0:T(8,128)(2,1)} %bitcast.4, bf16[8,2,256,256]{3,2,1,0:T(8,128)(2,1)} %left.1, bf16[8,2,256,256]{3,2,1,0:T(8,128)(2,1)} %right.1, f32[12,4,4]{2,1,0:T(4,128)} %copy.11.left_op, f32[12,4,4]{2,1,0:T(4,128)} %copy.12.right_op, s32[8]{0:T(128)} %term_ref.1, s32[4]{0:T(128)} %order_ref.1, ...), custom_call_target="tpu_custom_call" | custom-call | flops 25769803776 | bytes 16777216 | tf_op jit(solution)/shard_map/pallas_call | solution.py:283
  88.6 2.4 %copy.13 = bf16[32,2,4096]{2,1,0:T(2,128)(2,1)} copy(bf16[32,2,4096]{2,0,1:T(8,128)(2,1)} %bitcast.5) | data formatting | bytes 1048576 | tf_op jit(solution)/shard_map/transpose | solution.py:329

commit v3 on v1

--- a/solution.py
+++ b/solution.py
@@ -174,34 +174,20 @@
             line_out[i] = (own_part[i] + pair_in[i].astype(jnp.float32)).astype(jnp.bfloat16)
             line_copy(i).start()
 
-    def step(i, carry):
-        k = lax.div(i, outer)
-        j = lax.rem(i, outer)
-
-        @pl.when(j == 0)
-        def _():
-            apply_left(k, i == 0)
-
-        dest = lax.rem(far + 1 + j, outer) * INNER
-        pair_out[i] = rows_for(k, dest + (1 - near)).astype(jnp.bfloat16)
-        pair_copy(i).start()
-        own_part[i] = rows_for(k, dest + near)
-
-        @pl.when(i >= 1)
-        def _():
-            combine(i - 1)
-
-        return carry
-
-    lax.fori_loop(0, steps, step, 0)
-    combine(steps - 1)
-
-    out_row = lax.broadcasted_iota(jnp.int32, (SUB, bond), 0)
-    out_col = lax.broadcasted_iota(jnp.int32, (SUB, bond), 1)
-    for k in range(slots):
+    def add_lines(k):
         mine = k * outer + outer - 1
         for j in range(outer - 1):
             line_copy(k * outer + j).wait_recv()
+        total = own_part[mine]
+        for j in range(outer - 1):
+            total = total + line_in[k * outer + j].astype(jnp.float32)
+        own_part[mine] = total
+
+    out_row = lax.broadcasted_iota(jnp.int32, (SUB, bond), 0)
+    out_col = lax.broadcasted_iota(jnp.int32, (SUB, bond), 1)
+
+    def finish(k):
+        mine = k * outer + outer - 1
         sector = order_ref[base + k]
         size_left = left_size_ref[sector]
         size_right = right_size_ref[sector]
@@ -210,11 +196,40 @@
             for p in range(states):
                 rows = pl.ds(b * tile + p * SUB, SUB)
                 total = own_part[mine, rows] + pair_in[mine, rows].astype(jnp.float32)
-                for j in range(outer - 1):
-                    total = total + line_in[k * outer + j, rows].astype(jnp.float32)
                 out[k, pl.ds(b * SUB, SUB), pl.ds(p * bond, bond)] = jnp.where(
                     keep, total, 0.0
                 ).astype(jnp.bfloat16)
+
+    def step(i, carry):
+        k = lax.div(i, outer)
+        j = lax.rem(i, outer)
+
+        @pl.when(j == 0)
+        def _():
+            apply_left(k, i == 0)
+
+        dest = lax.rem(far + 1 + j, outer) * INNER
+        pair_out[i] = rows_for(k, dest + (1 - near)).astype(jnp.bfloat16)
+        pair_copy(i).start()
+        own_part[i] = rows_for(k, dest + near)
+
+        @pl.when(i >= 1)
+        def _():
+            combine(i - 1)
+
+        for done in range(slots - 1):
+
+            @pl.when(i == (done + 1) * outer + min(2, outer - 1))
+            def _():
+                add_lines(done)
+                finish(done)
+
+        return carry
+
+    lax.fori_loop(0, steps, step, 0)
+    add_lines(slots - 1)
+    combine(steps - 1)
+    finish(slots - 1)
 
     for sent, _ in wave_copies:
         sent.wait_send()

time: 87.6 us -> 87.6 us (level)
  no operation moved by 1% of the time
where the time goes in v3:
time: 87.6 us; the launch traced here: 86.4 us
  Pallas kernels  73.8 us (84%)
  local copies, waits for them, and re-layouts  10.8 us (12%)
  matrix products  1.74 us (2%)
    pallas_call x1, Pallas kernels, local(): pl.pallas_call(functools.partial(kernel, (terms, slots, bond, states, ops...  73.8 us
    unnamed x3, local copies, waits for them, and re-layouts  7.73 us
    transpose x1, local copies, waits for them, and re-layouts, local(): return jnp.transpose(result, (1, 0, 2))  2.38 us

profile of v3, /device:TPU:0, one launch (start us, length us, event | category | flops | bytes accessed | tf_op | source)
XLA Modules:
  0.0 86.4 jit_solution(1697798321772833733)
XLA Ops:
  0.0 0.0 copy-start
  0.0 0.7 copy-done
  0.7 0.8 fusion.1
  1.5 0.9 %fusion = f32[8,16]{0,1:S(1)} fusion(f32[12,16]{0,1:T(8,128)} %bitcast.17, s32[8]{0:T(128)} %param.14), kind=kOutput, calls=%fused_computation.3 | convolution fusion | flops 18528 | bytes 1312
  2.5 0.7 copy.15.table
  3.2 7.0 %copy.18 = bf16[256,2,4096]{2,0,1:T(8,128)(2,1)} copy(bf16[256,2,4096]{2,1,0:T(2,128)(2,1)} %param.9) | data formatting | bytes 8388608 | tf_op args[0]
  10.2 73.8 %shard_map.91 = bf16[2,32,4096]{2,1,0:T(8,128)(2,1)} custom-call(bf16[2,256,4096]{2,1,0:T(8,128)(2,1)} %bitcast.12, bf16[8,2,256,256]{3,2,1,0:T(8,128)(2,1)} %left.1, bf16[8,2,256,256]{3,2,1,0:T(8,128)(2,1)} %right.1, bf16[8,16,16]{2,1,0:T(8,128)(2,1)} %copy.15.table, s32[4]{0:T(128)} %order_ref.1, s32[4]{0:T(128)} %left_size_ref.1, s32[4]{0:T(128)} %right_size_ref.1), custom_call_target="tpu_custom_call" | custom-call | flops 25769803776 | bytes 16777216 | tf_op jit(solution)/shard_map/pallas_call | solution.py:286
  84.0 2.4 %copy.16 = bf16[32,2,4096]{2,1,0:T(2,128)(2,1)} copy(bf16[32,2,4096]{2,0,1:T(8,128)(2,1)} %bitcast.13) | data formatting | bytes 1048576 | tf_op jit(solution)/shard_map/transpose | solution.py:321
  (1 shorter events, 0.0 us)
Async XLA Ops:
  0.0 0.7 copy-start
